TPU v7x, 32 devices: a whole 2x2x4 slice. The times are simulated.
32 devices in a mesh: groups: 2 (over y), blk: 4 (over z), dp: 2 (over x), sub: 2 (over core).
Axes of the slice: x: 2, y: 2, z: 4, core: 2. Of those that a mesh axis runs over, the one named last changes fastest.
Arguments:
- cls_feats: bfloat16 [4096, 1024], P(('groups', 'blk', 'dp', 'sub')), parts along dimension 0, may hold values from -6 to 6
- proj: bfloat16 [1024, 768], replicated, may hold values from -0.1875 to 0.1875
- cluster_id: int32 [4096, 1], P(('groups', 'blk', 'dp', 'sub')), parts along dimension 0, may hold values from 0 to 7; in each aligned block of 128 rows (0 to 127, 128 to 255, ...) at most 32 rows name the same one
- row_index: int32 [4096], P(('groups', 'blk', 'dp', 'sub')), parts along dimension 0, may hold values from 0 to 2047, each once
- assign: int32 [16], P('groups'), parts along dimension 0, may hold values from 0 to 7, each once
Outputs:
- best_cos: float32 [4096], P(('groups', 'blk', 'dp', 'sub')), parts along dimension 0
There are 2 independent parts, one for each index of `groups`. A program takes and returns all parts, laid end to end along the dimension named above; an argument that names none is the same for every part. Nothing has to cross between parts.
Inputs may be any that keep to these rules, and one draw needn't show every extreme that they name: `cluster_id`: among the 128 images of one device, at most 32 lie in one fine cluster; some device has exactly 32 in some fine cluster, and every fine cluster has some image. `row_index`: every number appears once. `assign`: every number appears once.
All inputs are finite; a program needn't handle non-finite values.
Results may differ from a plain program's by a relative error of at most 0.0015.
Values may be sent and summed in bfloat16 or wider, within the bound.
A program may use at most 64 MiB of HBM per device.

v0:
```python
import math

import jax
import jax.numpy as jnp
from jax import lax
from jax.sharding import PartitionSpec as P

empty_mark = 2**30


def fold_best(carry, piece, row_emb, row_idx):
    col_emb, col_idx = piece
    count = col_emb.shape[0]
    width = math.gcd(count, 1024)
    blocks = count // width
    col_blocks = col_emb.reshape(blocks, width, col_emb.shape[1])
    idx_blocks = col_idx.reshape(blocks, width)

    def step(best, pair):
        block_emb, block_idx = pair
        scores = lax.dot_general(
            row_emb, block_emb, (((1,), (1,)), ((), ())), preferred_element_type=jnp.float32
        )
        scores = jnp.where(block_idx[None, :] < row_idx[:, None], scores, -1.0)
        return (jnp.maximum(best, jnp.max(scores, axis=1)), None)

    best, _ = lax.scan(step, carry, (col_blocks, idx_blocks))
    return best


def local(cls_feats, proj, cluster_id, row_index, assign):
    rows = cls_feats.shape[0]
    feats = cls_feats.astype(jnp.float32)
    center = jnp.mean(feats, axis=1, keepdims=True)
    spread = jnp.mean((feats - center) ** 2, axis=1, keepdims=True)
    normed = ((feats - center) * lax.rsqrt(spread + 1e-05)).astype(jnp.bfloat16)
    proj_out = jnp.dot(normed, proj, preferred_element_type=jnp.float32)
    scale = lax.rsqrt(jnp.sum(proj_out * proj_out, axis=1, keepdims=True) + 1e-06)
    emb = (proj_out * scale).astype(jnp.bfloat16)
    width = emb.shape[1]
    fine_count = assign.shape[0]
    most_fine = 2 * rows // fine_count
    slots = fine_count * most_fine
    onehot = cluster_id == jnp.arange(fine_count, dtype=jnp.int32)[None, :]
    counts = onehot.astype(jnp.int32)
    earlier = jnp.cumsum(counts, axis=0) - counts
    rank = jnp.sum(jnp.where(onehot, earlier, 0), axis=1)
    base = jnp.sum(jnp.where(onehot, assign[None, :], 0), axis=1)
    slot = base * most_fine + rank
    place = slot[None, :] == jnp.arange(slots, dtype=jnp.int32)[:, None]
    send_emb = jnp.dot(place.astype(jnp.bfloat16), emb, preferred_element_type=jnp.float32).astype(
        jnp.bfloat16
    )
    filled = jnp.any(place, axis=1)
    send_idx = jnp.where(
        filled, jnp.sum(jnp.where(place, row_index[None, :], 0), axis=1), empty_mark
    )
    n_groups = lax.axis_size("dp")
    per_group = slots // n_groups
    recv_emb, recv_idx = (
        lax.all_to_all(
            send_emb.reshape(n_groups, per_group, width),
            "dp",
            split_axis=0,
            concat_axis=0,
            tiled=True,
        ),
        lax.all_to_all(
            send_idx.reshape(n_groups, per_group), "dp", split_axis=0, concat_axis=0, tiled=True
        ),
    )
    own_emb = recv_emb.reshape(slots, width)
    own_idx = recv_idx.reshape(slots)
    both_emb, both_idx = (
        lax.all_gather(own_emb, "sub", axis=0, tiled=True),
        lax.all_gather(own_idx, "sub", axis=0, tiled=True),
    )
    start_best = jnp.full((2 * slots,), -1.0, jnp.float32)
    partial_best = fold_best(
        start_best,
        (
            lax.all_gather(own_emb, "blk", axis=0, tiled=True),
            lax.all_gather(own_idx, "blk", axis=0, tiled=True),
        ),
        both_emb,
        both_idx,
    )
    joined = lax.pmax(partial_best, "sub")
    best = lax.dynamic_slice_in_dim(joined, lax.axis_index("sub") * slots, slots, 0)
    back = lax.all_to_all(
        best.reshape(n_groups, per_group), "dp", split_axis=0, concat_axis=0, tiled=True
    )
    flat = back.reshape(slots)
    return jnp.dot(flat, place.astype(jnp.float32), precision=lax.Precision.HIGHEST)


def solution(mesh):
    in_specs = (
        P(("groups", "blk", "dp", "sub"), None),
        P(),
        P(("groups", "blk", "dp", "sub"), None),
        P(("groups", "blk", "dp", "sub")),
        P("groups"),
    )
    out_specs = P(("groups", "blk", "dp", "sub"))
    return jax.shard_map(local, mesh=mesh, in_specs=in_specs, out_specs=out_specs, check_vma=False)
```

profile of v0, /device:TPU:0, one launch (start us, length us, event | category | flops | bytes accessed | tf_op | source)
XLA Modules:
  0.0 79.7 jit_solution(8569290460033763673)
XLA Ops:
  6.5 0.9 %fusion.12 = s32[128,8]{1,0:T(8,128)S(1)} fusion(s32[128]{0:T(128)} %bitcast.25), kind=kLoop, calls=%fused_computation.23 | loop fusion | flops 2048 | bytes 4608 | tf_op jit(solution)/shard_map/convert_element_type | solution.py:45
  7.4 1.1 %convert_reduce_fusion = f32[128]{0:T(128)S(1)} fusion(bf16[128,1024]{1,0:T(8,128)(2,1)} %param.5), kind=kLoop, calls=%fused_computation.4 | loop fusion | flops 262016 | bytes 262656 | tf_op jit(solution)/shard_map/reduce_sum | solution.py:34
  8.5 1.2 %fusion.2 = f32[128]{0:T(128)S(1)} fusion(bf16[128,1024]{1,0:T(8,128)(2,1)} %param.5, f32[128]{0:T(128)S(1)} %broadcast_multiply_fusion), kind=kLoop, calls=%fused_computation.7 | loop fusion | flops 524160 | bytes 263168 | tf_op jit(solution)/shard_map/reduce_sum | solution.py:35
  9.7 1.5 %multiply_reduce_fusion = (f32[128]{0:T(128)S(1)}, f32[128,768]{1,0:T(8,128)S(1)}) fusion(bf16[1024,768]{1,0:T(8,128)(2,1)S(1)} %copy-done, bf16[128,1024]{1,0:T(8,128)(2,1)} %param.5, f32[128]{0:T(128)S(1)} %add_rsqrt_fusion.1, f32[128]{0:T(128)S(1)} %broadcast_multiply_fusion), kind=kOutput, calls=%fused_computation.10 | convolution fusion | flops 202047360 | bytes 2229760 | tf_op jit(solution)/shard_map/dot_general | solution.py:37
  11.1 0.0 copy-start.3
  11.1 0.2 reduce_window_sum.11
  11.3 0.2 select_reduce_fusion.3
  11.5 0.3 convolution_convert_fusion
  11.9 11.1 %all_to_all.20 = bf16[2,128,768]{2,1,0:T(8,128)(2,1)} all-to-all(bf16[2,128,768]{2,1,0:T(8,128)(2,1)S(1)} %bitcast.20), channel_id=1, replica_groups=mesh['groups'=2,'blk'=4,'dp'=2,'sub'=2] {'dp'}, dimensions={0} | all-to-all | bytes 786432 | tf_op jit(solution)/shard_map/all_to_all | solution.py:61
  23.0 0.0 all-gather.4.cloned.1.call-update
  23.0 0.1 fusion.9
  23.2 0.1 select_reduce_fusion.1
  23.3 0.6 broadcast_select_fusion
  23.9 3.2 %all-to-all-start = ((s32[2,1,128]{2,1,0:T(1,128)}), s32[2,1,128]{2,1,0:T(1,128)S(1)}, u32[]{:S(2)}, u32[]{:S(2)}) async-start(s32[2,1,128]{2,1,0:T(1,128)} %bitcast.1), calls=%async_computation | async-start | bytes 2048 | tf_op jit(solution)/shard_map/all_to_all | solution.py:68
  27.0 3.7 %all-to-all-done = s32[2,1,128]{2,1,0:T(1,128)S(1)} async-done(((s32[2,1,128]{2,1,0:T(1,128)}), s32[2,1,128]{2,1,0:T(1,128)S(1)}, u32[]{:S(2)}, u32[]{:S(2)}) %all-to-all-start) | async-done | bytes 1056 | tf_op jit(solution)/shard_map/all_to_all | solution.py:68
  30.8 1.8 %all-gather.1 = s32[2,1,256]{2,1,0:T(1,128)S(1)} all-gather(s32[1,1,256]{2,1,0:T(1,128)S(1)} %bitcast.21), channel_id=1, replica_groups=mesh['groups'=2,'blk'=4,'dp'=2,'sub'=2] {'sub'}, dimensions={0}, use_global_device_ids=true | all-gather | bytes 3072 | tf_op jit(solution)/shard_map/all_gather | solution.py:76
  32.5 11.6 %all-gather = s32[4,1,256]{2,1,0:T(1,128)S(1)} all-gather(s32[1,1,256]{2,1,0:T(1,128)S(1)} %bitcast.22), channel_id=1, replica_groups=mesh['groups'=2,'blk'=4,'dp'=2,'sub'=2] {'blk'}, dimensions={0}, use_global_device_ids=true | all-gather | bytes 5120 | tf_op jit(solution)/shard_map/all_gather | solution.py:83
  44.1 2.6 %all_gather.14 = bf16[512,768]{1,0:T(8,128)(2,1)S(1)} all-gather(bf16[256,768]{1,0:T(8,128)(2,1)} %bitcast.19), channel_id=1, replica_groups=mesh['groups'=2,'blk'=4,'dp'=2,'sub'=2] {'sub'}, dimensions={0}, use_global_device_ids=true | all-gather | bytes 1179648 | tf_op jit(solution)/shard_map/all_gather | solution.py:75
  46.7 14.2 %all-gather.4.cloned.1.call-done = bf16[1024,768]{1,0:T(8,128)(2,1)} async-done(((bf16[256,768]{1,0:T(8,128)(2,1)}), bf16[1024,768]{1,0:T(8,128)(2,1)}) %all-gather.4.cloned.1.call-update) | async-done | bytes 1572880 | tf_op jit(solution)/shard_map/all_gather | solution.py:82
  60.9 2.5 %select_reduce_fusion = f32[512]{0:T(512)S(1)} fusion(bf16[512,768]{1,0:T(8,128)(2,1)S(1)} %all_gather.14, bf16[1024,768]{1,0:T(8,128)(2,1)} %all-gather.4.cloned.1.call-done, s32[1024]{0:T(1024)S(1)} %bitcast.23, s32[512]{0:T(512)S(1)} %bitcast.27), kind=kOutput, calls=%fused_computation | convolution fusion | flops 806878720 | bytes 2367488 | tf_op jit(solution)/shard_map/while/body/eval_jaxpr/dot_general | solution.py:21
  63.4 2.5 %pmax.7 = f32[512]{0:T(512)S(1)} all-reduce(f32[512]{0:T(512)S(1)} %broadcast_maximum_fusion), channel_id=1, replica_groups=mesh['groups'=2,'blk'=4,'dp'=2,'sub'=2] {'sub'}, use_global_device_ids=true, to_apply=%region_9.10 | all-reduce | flops 512 | bytes 4096 | tf_op jit(solution)/shard_map/pmax | solution.py:88
  65.9 0.1 dynamic_slice.9
  66.0 6.3 %all_to_all.21 = f32[2,1,128]{2,1,0:T(1,128)S(1)} all-to-all(f32[2,1,128]{2,1,0:T(1,128)S(1)} %bitcast.24), channel_id=1, replica_groups=mesh['groups'=2,'blk'=4,'dp'=2,'sub'=2] {'dp'}, dimensions={0} | all-to-all | bytes 2048 | tf_op jit(solution)/shard_map/all_to_all | solution.py:90
  72.2 0.7 convolution_bitcast_fusion
  (13 shorter events, 0.0 us)
Async XLA Ops:
  6.5 3.1 %copy-start = (bf16[1024,768]{1,0:T(8,128)(2,1)S(1)}, bf16[1024,768]{1,0:T(8,128)(2,1)}, u32[]{:S(2)}) copy-start(bf16[1024,768]{1,0:T(8,128)(2,1)} %param.6) | copy-start | bytes 4718596
  6.5 4.8 %copy-start.1 = (s32[128,1]{0,1:T(1,128)S(1)}, s32[128,1]{0,1:T(1,128)}, u32[]{:S(2)}) copy-start(s32[128,1]{0,1:T(1,128)} %param.7) | copy-start | bytes 1540
  6.5 4.8 %copy-start.2 = (s32[8]{0:T(128)S(1)}, s32[8]{0:T(128)}, u32[]{:S(2)}) copy-start(s32[8]{0:T(128)} %param.9) | copy-start | bytes 100
  6.5 54.4 %all-gather.4.cloned.1.call-start = ((), (), s32[]{:S(2)}) async-start(), calls=%async_computation.3 | async-start | bytes 1966080 | tf_op jit(solution)/shard_map/all_gather | solution.py:82
  11.1 12.0 %copy-start.3 = (s32[128]{0:T(128)S(1)}, s32[128]{0:T(128)}, u32[]{:S(2)}) copy-start(s32[128]{0:T(128)} %param.8) | copy-start | bytes 1540
  23.9 6.9 %all-to-all-start = ((s32[2,1,128]{2,1,0:T(1,128)}), s32[2,1,128]{2,1,0:T(1,128)S(1)}, u32[]{:S(2)}, u32[]{:S(2)}) async-start(s32[2,1,128]{2,1,0:T(1,128)} %bitcast.1), calls=%async_computation | async-start | bytes 2048 | tf_op jit(solution)/shard_map/all_to_all | solution.py:68
Sparse Core Ops, SparseCore 0:
  23.1 37.7 all-gather.3
where the time goes:
time: 80.1 us; the launch traced here: 79.7 us
  blocking collectives  35.8 us (45%)
  waiting for transfers between devices  17.9 us (22%)
  between operations  13.5 us (17%)
  matrix products  4.95 us (6%)
  other arithmetic  4.3 us (5%)
  starting transfers between devices  3.16 us (4%)
    all_gather x1, waiting for transfers between devices, local(): lax.all_gather(own_emb, 'blk', axis=0, tiled=True)  14.2 us
    all_gather x1, blocking collectives, local(): lax.all_gather(own_idx, 'blk', axis=0, tiled=True)  11.6 us
    all_to_all x1, blocking collectives, local(): lax.all_to_all(send_emb.reshape(n_groups, per_group, width), 'dp', split_...  11.1 us
    all_to_all x1, blocking collectives, local(): lax.all_to_all(best.reshape(n_groups, per_group), 'dp', split_axis=0, con...  6.27 us
    all_to_all x1, waiting for transfers between devices, local(): lax.all_to_all(send_idx.reshape(n_groups, per_group), 'dp', split_axis=0,...  3.73 us
    all_to_all x1, starting transfers between devices, local(): lax.all_to_all(send_idx.reshape(n_groups, per_group), 'dp', split_axis=0,...  3.16 us
    all_gather x1, blocking collectives, local(): lax.all_gather(own_emb, 'sub', axis=0, tiled=True)  2.57 us
    dot_general x1, matrix products, step(): lax.dot_general(row_emb, block_emb, (((1,), (1,)), ((), ())), preferred_e...  2.5 us
  transfers between devices with their start and end apart: 2, of which 2 were waited for; matrix products, arithmetic and copies ran while one was open for 1% of the time, Pallas kernels for 0%

commit v1 on v0

v1 whole, which is shorter than its diff:
```python
import functools

import jax
import jax.numpy as jnp
from jax import lax
from jax.experimental import pallas as pl
from jax.experimental.pallas import tpu as pltpu
from jax.sharding import PartitionSpec as P

MESH = pl.DeviceIdType.MESH
NT = (((1,), (1,)), ((), ()))


def each(start, stop, body):
    if stop - start <= 4:
        for i in range(start, stop):
            body(i)
    else:
        lax.fori_loop(start, stop, lambda i, _: (body(i), None)[1], None)


def kernel(
    n_blk, n_dp, n_sub, images,
    feats_hbm, proj_hbm, cid_ref, idx_ref, assign_ref,
    out_ref,
    feats_ref, proj_ref, plane, plane_key, far, far_key, part_out, part_in, ret_out, ret_in,
    load_sem, pe_send, pe_recv, pk_send, pk_recv, fe_send, fe_recv, fk_send, fk_recv,
    po_send, po_recv, re_send, re_recv,
):
    n_plane = n_dp * n_sub
    n_far = n_blk // 2
    whole_far = (n_blk - 1) // 2
    z, x, c = lax.axis_index("blk"), lax.axis_index("dp"), lax.axis_index("sub")
    rows = idx_ref.shape[1]

    def in_plane(k, sign):
        dx, dc = lax.div(k, n_sub), lax.rem(k, n_sub)
        if sign < 0:
            dx, dc = n_dp - dx, n_sub - dc
        return {"blk": z, "dp": lax.rem(x + dx, n_dp), "sub": lax.rem(c + dc, n_sub)}

    def across(d, sign):
        return {"blk": lax.rem(z + (d if sign > 0 else n_blk - d), n_blk), "dp": x, "sub": c}

    half = n_blk // 2
    lower = z < half
    within = jnp.where(lower, z, z - half)
    sends_half = (lax.rem(within, 2) == 0) == lower
    has_half = n_far > whole_far

    load_feats = pltpu.make_async_copy(feats_hbm, feats_ref, load_sem.at[0])
    load_proj = pltpu.make_async_copy(proj_hbm, proj_ref, load_sem.at[1])
    load_feats.start()
    load_proj.start()

    barrier = pltpu.get_barrier_semaphore()

    def greet(device):
        pl.semaphore_signal(barrier, inc=1, device_id=device, device_id_type=MESH)

    each(1, n_plane, lambda k: greet(in_plane(k, 1)))

    def greet_far(d):
        greet(across(d, 1))
        greet(across(d, -1))

    each(1, whole_far + 1, greet_far)
    if has_half:
        greet(across(half, 1))
    pl.semaphore_wait(barrier, n_plane - 1 + 2 * whole_far + (1 if has_half else 0))

    def remote(src, dst, send, recv, device):
        return pltpu.make_async_remote_copy(
            src_ref=src, dst_ref=dst, send_sem=send, recv_sem=recv,
            device_id=device, device_id_type=MESH,
        )

    def plane_emb_copy(k):
        return remote(plane.at[0], plane.at[k], pe_send.at[k], pe_recv.at[k], in_plane(k, 1))

    def plane_key_copy(k):
        return remote(plane_key.at[0], plane_key.at[k], pk_send.at[k], pk_recv.at[k], in_plane(k, 1))

    def far_emb_copy(d):
        return remote(plane.at[0], far.at[d - 1], fe_send.at[d - 1], fe_recv.at[d - 1], across(d, 1))

    def far_key_copy(d):
        return remote(plane_key.at[0], far_key.at[d - 1], fk_send.at[d - 1], fk_recv.at[d - 1], across(d, 1))

    def part_copy(k):
        return remote(part_out.at[k], part_in.at[k], po_send.at[k], po_recv.at[k], in_plane(k, -1))

    def ret_copy(d):
        return remote(ret_out.at[d - 1], ret_in.at[d - 1], re_send.at[d - 1], re_recv.at[d - 1], across(d, -1))

    per_coarse = assign_ref.shape[0] // n_dp
    cid = cid_ref[...]
    base = jnp.zeros_like(cid)
    for f in range(assign_ref.shape[0]):
        base = jnp.where(cid == f, lax.div(assign_ref[f], per_coarse) * images, base)
    key = base + idx_ref[...]
    sub_row = lax.broadcasted_iota(jnp.int32, (8, rows), 0)
    plane_key[0] = jnp.where(
        sub_row == 0, jnp.broadcast_to(key, (8, rows)), jnp.broadcast_to(base, (8, rows))
    )
    each(1, whole_far + 1, lambda d: far_key_copy(d).start())
    if has_half:
        pl.when(sends_half)(lambda: far_key_copy(half).start())
    each(1, n_plane, lambda k: plane_key_copy(k).start())

    load_feats.wait()
    feats = feats_ref[...].astype(jnp.float32)
    center = jnp.mean(feats, axis=1, keepdims=True)
    shifted = feats - center
    spread = jnp.mean(shifted * shifted, axis=1, keepdims=True)
    normed = (shifted * lax.rsqrt(spread + 1e-05)).astype(jnp.bfloat16)
    load_proj.wait()
    proj_out = jnp.dot(normed, proj_ref[...], preferred_element_type=jnp.float32)
    scale = lax.rsqrt(jnp.sum(proj_out * proj_out, axis=1, keepdims=True) + 1e-06)
    plane[0] = (proj_out * scale).astype(jnp.bfloat16)

    if has_half:
        pl.when(sends_half)(lambda: far_emb_copy(half).start())
    each(1, whole_far + 1, lambda d: far_emb_copy(d).start())
    each(1, n_plane, lambda k: plane_emb_copy(n_plane - k).start())

    def column(key_row):
        return jnp.transpose(jnp.broadcast_to(key_row, (rows, rows)))

    def lane_best(scores):
        return jnp.max(jnp.transpose(scores), axis=0, keepdims=True)

    def spread8(row):
        return jnp.broadcast_to(row, (8, rows))

    own_col = column(plane_key[0][0:1])

    def own_step(k, best):
        keys = plane_key[k]
        k_row, b_row = keys[0:1], keys[1:2]
        scores = lax.dot_general(plane[0], plane[k], NT, preferred_element_type=jnp.float32)
        good = (own_col >= b_row) & (own_col < b_row + images) & (own_col > k_row)
        return jnp.maximum(best, jnp.where(good, scores, -1.0))

    def arrived(k):
        plane_key_copy(k).wait_recv()
        plane_emb_copy(k).wait_recv()

    best = own_step(0, jnp.full((rows, rows), -1.0, jnp.float32))
    if n_plane <= 4:
        for k in range(1, n_plane):
            arrived(k)
            best = own_step(k, best)
    else:
        best = lax.fori_loop(1, n_plane, lambda k, b: (arrived(k), own_step(k, b))[1], best)
    total = lane_best(best)

    def far_step(d, first):
        far_key_copy(d).wait_recv()
        far_emb_copy(d).wait_recv()
        col = column(far_key[d - 1][0:1])

        def step(k, best):
            keys = plane_key[k]
            k_row, b_row = keys[0:1], keys[1:2]
            scores = lax.dot_general(far[d - 1], plane[k], NT, preferred_element_type=jnp.float32)
            scores = jnp.where((col >= b_row) & (col < b_row + images), scores, -1.0)
            low = col < k_row
            gain = spread8(jnp.max(jnp.where(low, scores, -1.0), axis=0, keepdims=True))
            if first:
                part_out[k] = gain
            else:
                part_out[k] = jnp.maximum(part_out[k], gain)
            return jnp.maximum(best, jnp.where(low, -1.0, scores))

        best = jnp.full((rows, rows), -1.0, jnp.float32)
        if n_plane <= 4:
            for k in range(n_plane):
                best = step(k, best)
        else:
            best = lax.fori_loop(0, n_plane, step, best)
        ret_out[d - 1] = spread8(lane_best(best))
        ret_copy(d).start()

    if whole_far == 0:
        part_out[...] = jnp.full(part_out.shape, -1.0, jnp.float32)
    else:
        far_step(1, True)
        each(2, whole_far + 1, lambda d: far_step(d, False))
    if has_half:
        pl.when(jnp.logical_not(sends_half))(lambda: far_step(half, False))
    each(1, n_plane, lambda k: part_copy(k).start())

    total = jnp.maximum(total, part_out[0][0:1])

    def take_part(k, total):
        part_copy(k).wait_recv()
        return jnp.maximum(total, part_in[k][0:1])

    def take_ret(d, total):
        ret_copy(d).wait_recv()
        return jnp.maximum(total, ret_in[d - 1][0:1])

    out_ref[...] = jnp.full(out_ref.shape, -1.0, jnp.float32)
    for d in range(1, whole_far + 1):
        total = take_ret(d, total)
    for k in range(1, n_plane):
        total = take_part(k, total)
    out_ref[...] = total
    if has_half:

        @pl.when(sends_half)
        def _():
            out_ref[...] = take_ret(half, out_ref[...])

    def sent_far(d):
        far_key_copy(d).wait_send()
        far_emb_copy(d).wait_send()

    def sent_plane(k):
        plane_key_copy(k).wait_send()
        plane_emb_copy(k).wait_send()
        part_copy(k).wait_send()

    each(1, whole_far + 1, sent_far)
    each(1, whole_far + 1, lambda d: ret_copy(d).wait_send())
    if has_half:
        pl.when(sends_half)(lambda: sent_far(half))
        pl.when(jnp.logical_not(sends_half))(lambda: ret_copy(half).wait_send())
    each(1, n_plane, sent_plane)


def local(n_blk, n_dp, n_sub, cls_feats, proj, cluster_id, row_index, assign):
    rows, depth = cls_feats.shape
    width = proj.shape[1]
    n_plane, n_far = n_dp * n_sub, max(1, n_blk // 2)
    images = rows * n_blk * n_plane
    vmem, dma = pltpu.VMEM, pltpu.SemaphoreType.DMA
    out = pl.pallas_call(
        functools.partial(kernel, n_blk, n_dp, n_sub, images),
        out_shape=jax.ShapeDtypeStruct((1, rows), jnp.float32),
        in_specs=[
            pl.BlockSpec(memory_space=pl.ANY),
            pl.BlockSpec(memory_space=pl.ANY),
            pl.BlockSpec(memory_space=vmem),
            pl.BlockSpec(memory_space=vmem),
            pl.BlockSpec(memory_space=pltpu.SMEM),
        ],
        out_specs=pl.BlockSpec(memory_space=vmem),
        scratch_shapes=[
            vmem((rows, depth), cls_feats.dtype),
            vmem((depth, width), proj.dtype),
            vmem((n_plane, rows, width), jnp.bfloat16),
            vmem((n_plane, 8, rows), jnp.int32),
            vmem((n_far, rows, width), jnp.bfloat16),
            vmem((n_far, 8, rows), jnp.int32),
            vmem((n_plane, 8, rows), jnp.float32),
            vmem((n_plane, 8, rows), jnp.float32),
            vmem((n_far, 8, rows), jnp.float32),
            vmem((n_far, 8, rows), jnp.float32),
            dma((2,)),
            *[dma((n_plane,))] * 4,
            *[dma((n_far,))] * 4,
            *[dma((n_plane,))] * 2,
            *[dma((n_far,))] * 2,
        ],
        compiler_params=pltpu.CompilerParams(
            collective_id=0, has_side_effects=True, vmem_limit_bytes=32 * 2**20
        ),
    )(cls_feats, proj, cluster_id.reshape(1, rows), row_index.reshape(1, rows), assign)
    return out.reshape(rows)


def solution(mesh):
    split = ("groups", "blk", "dp", "sub")
    in_specs = (P(split, None), P(), P(split, None), P(split), P("groups"))
    body = functools.partial(local, mesh.shape["blk"], mesh.shape["dp"], mesh.shape["sub"])
    return jax.shard_map(body, mesh=mesh, in_specs=in_specs, out_specs=P(split), check_vma=False)
```

time: 80.1 us -> 26.1 us (0.33)
  blocking collectives: 35.8 us -> 0 us
  Pallas kernels: 0 us -> 21 us
  waiting for transfers between devices: 17.9 us -> 0 us
  between operations: 13.5 us -> 0.01 us
  matrix products: 4.95 us -> 0 us
  local copies, waits for them, and re-layouts: 0.09 us -> 4.83 us
  other arithmetic: 4.3 us -> 0 us
  starting transfers between devices: 3.16 us -> 0 us
    pallas_call x0 -> x1, Pallas kernels: none -> 21 us  [local(): pl.pallas_call(functools.partial(kernel, n_blk, n_dp, n_sub, images), out...]
    all_to_all x2 -> x0, blocking collectives: 17.4 us -> none  [the longest x1 11.1 us: local(): lax.all_to_all(send_emb.reshape(n_groups, per_group, width), 'dp', split_...]
    all_gather x3 -> x0, blocking collectives: 16 us -> none  [the longest x1 11.6 us: local(): lax.all_gather(own_idx, 'blk', axis=0, tiled=True)]
    all_gather x1 -> x0, waiting for transfers between devices: 14.2 us -> none  [local(): lax.all_gather(own_emb, 'blk', axis=0, tiled=True)]
    dot_general x4 -> x0, matrix products: 4.95 us -> none  [the longest x1 2.5 us: step(): lax.dot_general(row_emb, block_emb, (((1,), (1,)), ((), ())), preferred_e...]
    unnamed x8 -> x11, local copies, waits for them, and re-layouts: 0.02 us -> 4.83 us
    all_to_all x1 -> x0, waiting for transfers between devices: 3.73 us -> none  [local(): lax.all_to_all(send_idx.reshape(n_groups, per_group), 'dp', split_axis=0,...]
    all_to_all x1 -> x0, starting transfers between devices: 3.16 us -> none  [local(): lax.all_to_all(send_idx.reshape(n_groups, per_group), 'dp', split_axis=0,...]
  transfers between devices with their start and end apart: 2 -> 0, of which waited for: 2 -> 0; matrix products, arithmetic and copies ran while one was open for 1% -> 0% of each run, Pallas kernels for 0% -> 0%
where the time goes in v1:
time: 26.1 us; the launch traced here: 25.9 us
  Pallas kernels  21 us (80%)
  local copies, waits for them, and re-layouts  4.83 us (19%)
    pallas_call x1, Pallas kernels, local(): pl.pallas_call(functools.partial(kernel, n_blk, n_dp, n_sub, images), out...  21 us
    unnamed x11, local copies, waits for them, and re-layouts  4.83 us

profile of v1, /device:TPU:0, one launch (start us, length us, event | category | flops | bytes accessed | tf_op | source)
XLA Modules:
  0.0 25.9 jit_solution(18333379370113873135)
XLA Ops:
  0.0 0.0 copy-start
  0.0 1.4 %copy-done = bf16[1024,768]{1,0:T(8,128)(2,1)S(1)} copy-done((bf16[1024,768]{1,0:T(8,128)(2,1)S(1)}, bf16[1024,768]{1,0:T(8,128)(2,1)}, u32[]{:S(2)}) %copy-start) | copy-done | bytes 1572888
  1.4 0.0 copy-start.1
  1.4 0.9 %copy-done.1 = bf16[128,1024]{1,0:T(8,128)(2,1)S(1)} copy-done((bf16[128,1024]{1,0:T(8,128)(2,1)S(1)}, bf16[128,1024]{1,0:T(8,128)(2,1)}, u32[]{:S(2)}) %copy-start.1) | copy-done | bytes 262168
  2.4 0.0 copy-start.2
  2.4 0.7 %copy-done.2 = s32[128,1]{0,1:T(1,128)S(1)} copy-done((s32[128,1]{0,1:T(1,128)S(1)}, s32[128,1]{0,1:T(1,128)}, u32[]{:S(2)}) %copy-start.2) | copy-done | bytes 536
  3.0 0.0 copy-start.3
  3.0 0.7 %copy-done.3 = s32[128]{0:T(128)S(1)} copy-done((s32[128]{0:T(128)S(1)}, s32[128]{0:T(128)}, u32[]{:S(2)}) %copy-start.3) | copy-done | bytes 536
  3.7 0.0 copy-start.4
  3.7 0.7 %copy-done.4 = s32[8]{0:T(128)S(1)} copy-done((s32[8]{0:T(128)S(1)}, s32[8]{0:T(128)}, u32[]{:S(2)}) %copy-start.4) | copy-done | bytes 56
  4.3 21.0 %shard_map.55 = f32[1,128]{1,0:T(1,128)S(1)} custom-call(bf16[128,1024]{1,0:T(8,128)(2,1)S(1)} %copy-done.1, bf16[1024,768]{1,0:T(8,128)(2,1)S(1)} %copy-done, s32[1,128]{1,0:T(1,128)S(1)} %bitcast.3, s32[1,128]{1,0:T(1,128)S(1)} %bitcast.4, s32[8]{0:T(128)S(1)} %copy-done.4), custom_call_target="tpu_custom_call" | custom-call | tf_op jit(solution)/shard_map/pallas_call | solution.py:239
  25.4 0.5 %copy.7 = f32[128]{0:T(128)} copy(f32[128]{0:T(128)S(1)} %bitcast.5) | data formatting | bytes 1024
Async XLA Ops:
  0.0 1.4 %copy-start = (bf16[1024,768]{1,0:T(8,128)(2,1)S(1)}, bf16[1024,768]{1,0:T(8,128)(2,1)}, u32[]{:S(2)}) copy-start(bf16[1024,768]{1,0:T(8,128)(2,1)} %proj_hbm.1) | copy-start | bytes 4718596
  1.4 0.9 %copy-start.1 = (bf16[128,1024]{1,0:T(8,128)(2,1)S(1)}, bf16[128,1024]{1,0:T(8,128)(2,1)}, u32[]{:S(2)}) copy-start(bf16[128,1024]{1,0:T(8,128)(2,1)} %feats_hbm.1) | copy-start | bytes 786436
  2.4 0.7 %copy-start.2 = (s32[128,1]{0,1:T(1,128)S(1)}, s32[128,1]{0,1:T(1,128)}, u32[]{:S(2)}) copy-start(s32[128,1]{0,1:T(1,128)} %param.7) | copy-start | bytes 1540
  3.0 0.7 %copy-start.3 = (s32[128]{0:T(128)S(1)}, s32[128]{0:T(128)}, u32[]{:S(2)}) copy-start(s32[128]{0:T(128)} %param.8) | copy-start | bytes 1540
  3.7 0.7 %copy-start.4 = (s32[8]{0:T(128)S(1)}, s32[8]{0:T(128)}, u32[]{:S(2)}) copy-start(s32[8]{0:T(128)} %assign_ref.1) | copy-start | bytes 100

commit v2 on v1

--- a/solution.py
+++ b/solution.py
@@ -21,9 +21,9 @@
 
 def kernel(
     n_blk, n_dp, n_sub, images,
-    feats_hbm, proj_hbm, cid_ref, idx_ref, assign_ref,
+    feats_hbm, proj_hbm, cid_hbm, idx_hbm, assign_hbm,
     out_ref,
-    feats_ref, proj_ref, plane, plane_key, far, far_key, part_out, part_in, ret_out, ret_in,
+    feats_ref, proj_ref, cid_ref, idx_ref, assign_ref, plane, plane_key, far, far_key, part_out, part_in, ret_out, ret_in,
     load_sem, pe_send, pe_recv, pk_send, pk_recv, fe_send, fe_recv, fk_send, fk_recv,
     po_send, po_recv, re_send, re_recv,
 ):
@@ -48,10 +48,15 @@
     sends_half = (lax.rem(within, 2) == 0) == lower
     has_half = n_far > whole_far
 
-    load_feats = pltpu.make_async_copy(feats_hbm, feats_ref, load_sem.at[0])
-    load_proj = pltpu.make_async_copy(proj_hbm, proj_ref, load_sem.at[1])
-    load_feats.start()
-    load_proj.start()
+    loads = [
+        pltpu.make_async_copy(src, dst, load_sem.at[i])
+        for i, (src, dst) in enumerate((
+            (assign_hbm, assign_ref), (cid_hbm, cid_ref), (idx_hbm, idx_ref),
+            (feats_hbm, feats_ref), (proj_hbm, proj_ref),
+        ))
+    ]
+    for load in loads:
+        load.start()
 
     barrier = pltpu.get_barrier_semaphore()
 
@@ -93,6 +98,8 @@
     def ret_copy(d):
         return remote(ret_out.at[d - 1], ret_in.at[d - 1], re_send.at[d - 1], re_recv.at[d - 1], across(d, -1))
 
+    for load in loads[:3]:
+        load.wait()
     per_coarse = assign_ref.shape[0] // n_dp
     cid = cid_ref[...]
     base = jnp.zeros_like(cid)
@@ -108,13 +115,13 @@
         pl.when(sends_half)(lambda: far_key_copy(half).start())
     each(1, n_plane, lambda k: plane_key_copy(k).start())
 
-    load_feats.wait()
+    loads[3].wait()
     feats = feats_ref[...].astype(jnp.float32)
     center = jnp.mean(feats, axis=1, keepdims=True)
     shifted = feats - center
     spread = jnp.mean(shifted * shifted, axis=1, keepdims=True)
     normed = (shifted * lax.rsqrt(spread + 1e-05)).astype(jnp.bfloat16)
-    load_proj.wait()
+    loads[4].wait()
     proj_out = jnp.dot(normed, proj_ref[...], preferred_element_type=jnp.float32)
     scale = lax.rsqrt(jnp.sum(proj_out * proj_out, axis=1, keepdims=True) + 1e-06)
     plane[0] = (proj_out * scale).astype(jnp.bfloat16)
@@ -239,17 +246,14 @@
     out = pl.pallas_call(
         functools.partial(kernel, n_blk, n_dp, n_sub, images),
         out_shape=jax.ShapeDtypeStruct((1, rows), jnp.float32),
-        in_specs=[
-            pl.BlockSpec(memory_space=pl.ANY),
-            pl.BlockSpec(memory_space=pl.ANY),
-            pl.BlockSpec(memory_space=vmem),
-            pl.BlockSpec(memory_space=vmem),
-            pl.BlockSpec(memory_space=pltpu.SMEM),
-        ],
+        in_specs=[pl.BlockSpec(memory_space=pltpu.HBM)] * 5,
         out_specs=pl.BlockSpec(memory_space=vmem),
         scratch_shapes=[
             vmem((rows, depth), cls_feats.dtype),
             vmem((depth, width), proj.dtype),
+            vmem((1, rows), jnp.int32),
+            vmem((1, rows), jnp.int32),
+            pltpu.SMEM(assign.shape, jnp.int32),
             vmem((n_plane, rows, width), jnp.bfloat16),
             vmem((n_plane, 8, rows), jnp.int32),
             vmem((n_far, rows, width), jnp.bfloat16),
@@ -258,14 +262,14 @@
             vmem((n_plane, 8, rows), jnp.float32),
             vmem((n_far, 8, rows), jnp.float32),
             vmem((n_far, 8, rows), jnp.float32),
-            dma((2,)),
+            dma((5,)),
             *[dma((n_plane,))] * 4,
             *[dma((n_far,))] * 4,
             *[dma((n_plane,))] * 2,
             *[dma((n_far,))] * 2,
         ],
         compiler_params=pltpu.CompilerParams(
-            collective_id=0, has_side_effects=True, vmem_limit_bytes=32 * 2**20
+            collective_id=0, has_side_effects=True, vmem_limit_bytes=56 * 2**20
         ),
     )(cls_feats, proj, cluster_id.reshape(1, rows), row_index.reshape(1, rows), assign)
     return out.reshape(rows)

time: 26.1 us -> 22.3 us (0.85)
  local copies, waits for them, and re-layouts: 4.83 us -> 1.19 us
    unnamed x11 -> x1, local copies, waits for them, and re-layouts: 4.83 us -> 1.19 us
where the time goes in v2:
time: 22.3 us; the launch traced here: 22.1 us
  Pallas kernels  20.9 us (94%)
  local copies, waits for them, and re-layouts  1.19 us (5%)
    pallas_call x1, Pallas kernels, local(): pl.pallas_call(functools.partial(kernel, n_blk, n_dp, n_sub, images), out...  20.9 us
    unnamed x1, local copies, waits for them, and re-layouts  1.19 us

profile of v2, /device:TPU:0, one launch (start us, length us, event | category | flops | bytes accessed | tf_op | source)
XLA Modules:
  0.0 22.1 jit_solution(15973731436792444511)
XLA Ops:
  0.0 20.9 %shard_map.55 = f32[1,128]{1,0:T(1,128)} custom-call(bf16[128,1024]{1,0:T(8,128)(2,1)} %feats_hbm.1, bf16[1024,768]{1,0:T(8,128)(2,1)} %proj_hbm.1, s32[1,128]{1,0:T(1,128)} %bitcast.3, s32[1,128]{1,0:T(1,128)} %bitcast.4, s32[8]{0:T(128)} %assign_hbm.1), custom_call_target="tpu_custom_call" | custom-call | tf_op jit(solution)/shard_map/pallas_call | solution.py:246
  21.0 1.2 %copy.7 = f32[128]{0:T(128)} copy(f32[128]{0:T(128)} %bitcast.5) | data formatting | bytes 1024

commit v3 on v2

--- a/solution.py
+++ b/solution.py
@@ -245,7 +245,7 @@
     vmem, dma = pltpu.VMEM, pltpu.SemaphoreType.DMA
     out = pl.pallas_call(
         functools.partial(kernel, n_blk, n_dp, n_sub, images),
-        out_shape=jax.ShapeDtypeStruct((1, rows), jnp.float32),
+        out_shape=pltpu.VMEM((1, rows), jnp.float32),
         in_specs=[pl.BlockSpec(memory_space=pltpu.HBM)] * 5,
         out_specs=pl.BlockSpec(memory_space=vmem),
         scratch_shapes=[

time: 22.3 us -> 21 us (0.942)
  local copies, waits for them, and re-layouts: 1.19 us -> 0.51 us
  Pallas kernels: 20.9 us -> 20.3 us
    unnamed x1, local copies, waits for them, and re-layouts: 1.19 us -> 0.51 us
    pallas_call x1, Pallas kernels: 20.9 us -> 20.3 us  [local(): pl.pallas_call(functools.partial(kernel, n_blk, n_dp, n_sub, images), out...]
where the time goes in v3:
time: 21 us; the launch traced here: 20.9 us
  Pallas kernels  20.3 us (97%)
  local copies, waits for them, and re-layouts  0.51 us (2%)
    pallas_call x1, Pallas kernels, local(): pl.pallas_call(functools.partial(kernel, n_blk, n_dp, n_sub, images), out...  20.3 us
    unnamed x1, local copies, waits for them, and re-layouts  0.51 us

profile of v3, /device:TPU:0, one launch (start us, length us, event | category | flops | bytes accessed | tf_op | source)
XLA Modules:
  0.0 20.9 jit_solution(13494678805596663261)
XLA Ops:
  0.0 20.3 %shard_map.55 = f32[1,128]{1,0:T(1,128)S(1)} custom-call(bf16[128,1024]{1,0:T(8,128)(2,1)} %feats_hbm.1, bf16[1024,768]{1,0:T(8,128)(2,1)} %proj_hbm.1, s32[1,128]{1,0:T(1,128)} %bitcast.4, s32[1,128]{1,0:T(1,128)} %bitcast.5, s32[8]{0:T(128)} %assign_hbm.1), custom_call_target="tpu_custom_call" | custom-call | tf_op jit(solution)/shard_map/pallas_call | solution.py:246
  20.4 0.5 %copy.7 = f32[128]{0:T(128)} copy(f32[128]{0:T(128)S(1)} %bitcast.3) | data formatting | bytes 1024

commit v4 on v3

--- a/solution.py
+++ b/solution.py
@@ -86,8 +86,14 @@
     def plane_key_copy(k):
         return remote(plane_key.at[0], plane_key.at[k], pk_send.at[k], pk_recv.at[k], in_plane(k, 1))
 
-    def far_emb_copy(d):
-        return remote(plane.at[0], far.at[d - 1], fe_send.at[d - 1], fe_recv.at[d - 1], across(d, 1))
+    piece = rows // 2
+
+    def far_emb_copy(d, h):
+        part = pl.ds(h * piece, piece)
+        return remote(
+            plane.at[0, part], far.at[d - 1, part],
+            fe_send.at[d - 1, h], fe_recv.at[d - 1, h], across(d, 1),
+        )
 
     def far_key_copy(d):
         return remote(plane_key.at[0], far_key.at[d - 1], fk_send.at[d - 1], fk_recv.at[d - 1], across(d, 1))
@@ -127,8 +133,11 @@
     plane[0] = (proj_out * scale).astype(jnp.bfloat16)
 
     if has_half:
-        pl.when(sends_half)(lambda: far_emb_copy(half).start())
-    each(1, whole_far + 1, lambda d: far_emb_copy(d).start())
+        pl.when(sends_half)(lambda: far_emb_copy(half, 0).start())
+    each(1, whole_far + 1, lambda d: far_emb_copy(d, 0).start())
+    if has_half:
+        pl.when(sends_half)(lambda: far_emb_copy(half, 1).start())
+    each(1, whole_far + 1, lambda d: far_emb_copy(d, 1).start())
     each(1, n_plane, lambda k: plane_emb_copy(n_plane - k).start())
 
     def column(key_row):
@@ -164,28 +173,32 @@
 
     def far_step(d, first):
         far_key_copy(d).wait_recv()
-        far_emb_copy(d).wait_recv()
-        col = column(far_key[d - 1][0:1])
-
-        def step(k, best):
-            keys = plane_key[k]
-            k_row, b_row = keys[0:1], keys[1:2]
-            scores = lax.dot_general(far[d - 1], plane[k], NT, preferred_element_type=jnp.float32)
-            scores = jnp.where((col >= b_row) & (col < b_row + images), scores, -1.0)
-            low = col < k_row
-            gain = spread8(jnp.max(jnp.where(low, scores, -1.0), axis=0, keepdims=True))
-            if first:
-                part_out[k] = gain
+        whole_col = column(far_key[d - 1][0:1])
+        halves = []
+        for h in range(2):
+            far_emb_copy(d, h).wait_recv()
+            span = slice(h * piece, (h + 1) * piece)
+            col = whole_col[span]
+            fresh = first and h == 0
+
+            def step(k, best):
+                keys = plane_key[k]
+                k_row, b_row = keys[0:1], keys[1:2]
+                scores = lax.dot_general(far[d - 1, span], plane[k], NT, preferred_element_type=jnp.float32)
+                scores = jnp.where((col >= b_row) & (col < b_row + images), scores, -1.0)
+                low = col < k_row
+                gain = spread8(jnp.max(jnp.where(low, scores, -1.0), axis=0, keepdims=True))
+                part_out[k] = gain if fresh else jnp.maximum(part_out[k], gain)
+                return jnp.maximum(best, jnp.where(low, -1.0, scores))
+
+            best = jnp.full((piece, rows), -1.0, jnp.float32)
+            if n_plane <= 4:
+                for k in range(n_plane):
+                    best = step(k, best)
             else:
-                part_out[k] = jnp.maximum(part_out[k], gain)
-            return jnp.maximum(best, jnp.where(low, -1.0, scores))
-
-        best = jnp.full((rows, rows), -1.0, jnp.float32)
-        if n_plane <= 4:
-            for k in range(n_plane):
-                best = step(k, best)
-        else:
-            best = lax.fori_loop(0, n_plane, step, best)
+                best = lax.fori_loop(0, n_plane, step, best)
+            halves.append(best)
+        best = jnp.concatenate(halves, axis=0)
         ret_out[d - 1] = spread8(lane_best(best))
         ret_copy(d).start()
 
@@ -222,7 +235,8 @@
 
     def sent_far(d):
         far_key_copy(d).wait_send()
-        far_emb_copy(d).wait_send()
+        far_emb_copy(d, 0).wait_send()
+        far_emb_copy(d, 1).wait_send()
 
     def sent_plane(k):
         plane_key_copy(k).wait_send()
@@ -264,7 +278,8 @@
             vmem((n_far, 8, rows), jnp.float32),
             dma((5,)),
             *[dma((n_plane,))] * 4,
-            *[dma((n_far,))] * 4,
+            *[dma((n_far, 2))] * 2,
+            *[dma((n_far,))] * 2,
             *[dma((n_plane,))] * 2,
             *[dma((n_far,))] * 2,
         ],

time: 21 us -> 22.1 us (1.052)
  Pallas kernels: 20.3 us -> 21.4 us
    pallas_call x1, Pallas kernels: 20.3 us -> 21.4 us  [local(): pl.pallas_call(functools.partial(kernel, n_blk, n_dp, n_sub, images), out...]
where the time goes in v4:
time: 22.1 us; the launch traced here: 22 us
  Pallas kernels  21.4 us (97%)
  local copies, waits for them, and re-layouts  0.51 us (2%)
    pallas_call x1, Pallas kernels, local(): pl.pallas_call(functools.partial(kernel, n_blk, n_dp, n_sub, images), out...  21.4 us
    unnamed x1, local copies, waits for them, and re-layouts  0.51 us

profile of v4, /device:TPU:0, one launch (start us, length us, event | category | flops | bytes accessed | tf_op | source)
XLA Modules:
  0.0 22.0 jit_solution(720977653013936579)
XLA Ops:
  0.0 21.4 %shard_map.55 = f32[1,128]{1,0:T(1,128)S(1)} custom-call(bf16[128,1024]{1,0:T(8,128)(2,1)} %feats_hbm.1, bf16[1024,768]{1,0:T(8,128)(2,1)} %proj_hbm.1, s32[1,128]{1,0:T(1,128)} %bitcast.4, s32[1,128]{1,0:T(1,128)} %bitcast.5, s32[8]{0:T(128)} %assign_hbm.1), custom_call_target="tpu_custom_call" | custom-call | tf_op jit(solution)/shard_map/pallas_call | solution.py:260
  21.4 0.5 %copy.7 = f32[128]{0:T(128)} copy(f32[128]{0:T(128)S(1)} %bitcast.3) | data formatting | bytes 1024
